TPU v7x, 256 devices: a whole 4x4x8 slice. The times are simulated.
256 devices in a mesh: ctx: 32 (over z, y_hi, core), tp: 8 (over y_lo, x).
Axes of the slice: x: 4, y: 4 (y_hi: 2, y_lo: 2; y = y_hi * 2 + y_lo), z: 8, core: 2. Of those that a mesh axis runs over, the one named last changes fastest.
Arguments:
- sample_ids: int32 [128], replicated, may hold values from 0 to 7, never falling along the last dimension, each value on 1 to 32 neighbouring positions
- layer_input: bfloat16 [16384, 8192], P('ctx', 'tp'), may hold values from -6 to 6
- hidden_acts: bfloat16 [16384, 28672], P('ctx', 'tp'), may hold values from -6 to 6
- gate_grad: bfloat16 [16384, 28672], P('ctx', 'tp'), may hold values from -0.1796875 to 0.1796875
- up_grad: bfloat16 [16384, 28672], P('ctx', 'tp'), may hold values from -0.1796875 to 0.1796875
- output_grad: bfloat16 [16384, 8192], P('ctx', 'tp'), may hold values from -0.1796875 to 0.1796875
- input_basis: bfloat16 [8192, 64], P('tp'), may hold values from -0.0625 to 0.0625
- hidden_basis: bfloat16 [28672, 64], P('tp'), may hold values from -0.03125 to 0.03125
- gate_basis: bfloat16 [28672, 64], P('tp'), may hold values from -0.03125 to 0.03125
- up_basis: bfloat16 [28672, 64], P('tp'), may hold values from -0.03125 to 0.03125
- output_basis: bfloat16 [8192, 64], P('tp'), may hold values from -0.0625 to 0.0625
Outputs:
- sample_grads: float32 [3, 8, 4096], P(None, None, 'ctx')
Inputs may be any that keep to these rules, and one draw needn't show every extreme that they name: `sample_ids`: sample ids never fall from one block to the next; every sequence holds 1 to 32 blocks, one exactly 32.
All inputs are finite; a program needn't handle non-finite values.
Results may differ from a plain program's by a relative error of at most 0.0003.
Values sent between devices are 32-bit elements; how exact they have to be, the bound alone decides.
A program may use at most 64 MiB of HBM per device.

v0:
```python
import jax
import jax.numpy as jnp
from jax import lax
from jax.sharding import PartitionSpec as P

K = 64
SAMPLES = 8
BLOCK = 128


def project(data, basis):
    return jnp.dot(data, basis, preferred_element_type=jnp.float32)


def per_group(one_hot, output_side, input_side):
    groups = one_hot.shape[1]
    spread = (one_hot[:, :, None] * output_side[:, None, :]).reshape(output_side.shape[0], -1)
    summed = jnp.einsum("ta,tb->ab", spread, input_side, precision=lax.Precision.HIGHEST)
    return summed.reshape(groups, K * K)


def all_three(one_hot, pieces):
    return jnp.stack(
        [
            per_group(one_hot, pieces[2], pieces[0]),
            per_group(one_hot, pieces[3], pieces[0]),
            per_group(one_hot, pieces[4], pieces[1]),
        ]
    )


def body(
    sample_ids,
    layer_input,
    hidden_acts,
    gate_grad,
    up_grad,
    output_grad,
    input_basis,
    hidden_basis,
    gate_basis,
    up_basis,
    output_basis,
):
    tok_count = layer_input.shape[0]
    first_row = lax.axis_index("ctx") * tok_count
    low_terms = (
        project(layer_input, input_basis),
        project(hidden_acts, hidden_basis),
        project(gate_grad, gate_basis),
        project(up_grad, up_basis),
        project(output_grad, output_basis),
    )
    pieces = lax.psum((low_terms[0], low_terms[1], low_terms[2], low_terms[3], low_terms[4]), "tp")
    row_count = pieces[0].shape[0]
    positions = first_row + jnp.arange(row_count, dtype=jnp.int32)
    block_ids = positions // BLOCK
    n_blocks = sample_ids.shape[0]
    members = block_ids[:, None] == jnp.arange(n_blocks, dtype=jnp.int32)[None, :]
    owners = jnp.sum(jnp.where(members, sample_ids[None, :], 0), axis=1)
    one_hot = (owners[:, None] == jnp.arange(SAMPLES, dtype=jnp.int32)[None, :]).astype(jnp.float32)
    summed = lax.psum_scatter(all_three(one_hot, pieces), "ctx", scatter_dimension=2, tiled=True)
    return summed


def solution(mesh):
    return jax.shard_map(
        body,
        mesh=mesh,
        in_specs=(
            P(),
            P("ctx", "tp"),
            P("ctx", "tp"),
            P("ctx", "tp"),
            P("ctx", "tp"),
            P("ctx", "tp"),
            P("tp", None),
            P("tp", None),
            P("tp", None),
            P("tp", None),
            P("tp", None),
        ),
        out_specs=P(None, None, "ctx"),
        check_vma=False,
    )
```

profile of v0, /device:TPU:2, one launch (start us, length us, event | category | flops | bytes accessed | tf_op | source)
XLA Modules:
  0.0 228.9 jit_solution(13327632222622296752)
XLA Ops:
  6.5 0.0 copy-start
  6.5 0.0 copy-start.4
  6.5 0.0 all-reduce.3.cloned.1.call-start
  6.5 1.2 copy-done
  7.8 0.0 copy-start.1
  7.8 2.2 fusion.5
  9.9 0.0 copy-start.2
  9.9 0.0 copy-start.5
  9.9 4.2 %fusion.10 = f32[512,64]{0,1:T(8,128)} fusion(bf16[512,3584]{1,0:T(8,128)(2,1)} %param.13, bf16[3584,64]{0,1:T(8,128)(2,1)} %param.18), kind=kOutput, calls=%fused_computation.23 | convolution fusion | flops 234881024 | bytes 4259840 | tf_op jit(solution)/shard_map/dot_general | solution.py:12
  14.1 0.0 copy-done.4
  14.1 0.0 copy-done.1
  14.1 0.0 copy-start.3
  14.1 0.0 copy-start.6
  14.1 1.9 fusion.4
  16.0 0.0 copy-done.2
  16.0 0.0 copy-done.5
  16.0 0.0 copy-start.7
  16.0 1.9 fusion.7
  17.9 0.0 copy-done.3
  17.9 0.0 copy-done.6
  17.9 1.1 fusion.9
  19.0 0.0 all-reduce.3.cloned.1.call-update
  19.0 0.0 reduce-scatter.2.cloned.1.call-start
  19.1 0.0 copy-done.7
  19.1 0.2 select_reduce_fusion
  19.3 81.8 %all-reduce.3.cloned.1.call-done = (f32[512,64]{0,1:T(8,128)}, f32[512,64]{0,1:T(8,128)}, f32[512,64]{0,1:T(8,128)}, f32[512,64]{0,1:T(8,128)}, f32[512,64]{0,1:T(8,128)}) async-done(((f32[512,64]{0,1:T(8,128)}, f32[512,64]{0,1:T(8,128)}, f32[512,64]{0,1:T(8,128)}, f32[512,64]{0,1:T(8,128)}, f32[512,64]{0,1:T(8,128)}), (f32[512,64]{0,1:T(8,128)}, f32[512,64]{0,1:T(8,128)}, f32[512,64]{0,1:T(8,128)}, ...) | async-done | bytes 655376 | tf_op jit(solution)/shard_map/psum | solution.py:54
  101.2 1.3 broadcast_multiply_fusion.2
  102.5 1.9 fusion.6
  104.4 0.1 stack_reshape.9
  104.5 1.9 fusion.8
  106.4 0.1 stack_reshape.10
  106.5 1.9 fusion.11
  108.4 0.1 stack_reshape.11
  108.5 0.8 pad_maximum_fusion
  109.3 0.0 reduce-scatter.2.cloned.1.call-update
  109.3 112.8 %reduce-scatter.2.cloned.1.call-done = f32[3,8,128]{2,1,0:T(8,128)} async-done(((f32[3,8,4096]{2,1,0:T(8,128)}), f32[3,8,128]{2,1,0:T(8,128)}) %reduce-scatter.2.cloned.1.call-update) | async-done | bytes 12304 | tf_op jit(solution)/shard_map/reduce_scatter | solution.py:62
  (2 shorter events, 0.0 us)
Async XLA Ops:
  6.5 1.2 copy-start
  6.5 7.5 %copy-start.4 = (bf16[3584,64]{0,1:T(8,128)(2,1)S(1)}, bf16[3584,64]{0,1:T(8,128)(2,1)}, u32[]{:S(2)}) copy-start(bf16[3584,64]{0,1:T(8,128)(2,1)} %param.19) | copy-start | bytes 1376260
  6.5 94.6 %all-reduce.3.cloned.1.call-start = ((), (), s32[]{:S(2)}) async-start(), calls=%async_computation.2 | async-start | bytes 1310720 | tf_op jit(solution)/shard_map/psum | solution.py:54
  7.8 6.3 %copy-start.1 = (bf16[512,3584]{1,0:T(8,128)(2,1)S(1)}, bf16[512,3584]{1,0:T(8,128)(2,1)}, u32[]{:S(2)}) copy-start(bf16[512,3584]{1,0:T(8,128)(2,1)} %param.14) | copy-start | bytes 11010052
  9.9 6.1 %copy-start.2 = (bf16[512,3584]{1,0:T(8,128)(2,1)S(1)}, bf16[512,3584]{1,0:T(8,128)(2,1)}, u32[]{:S(2)}) copy-start(bf16[512,3584]{1,0:T(8,128)(2,1)} %param.15) | copy-start | bytes 11010052
  9.9 6.1 %copy-start.5 = (bf16[3584,64]{0,1:T(8,128)(2,1)S(1)}, bf16[3584,64]{0,1:T(8,128)(2,1)}, u32[]{:S(2)}) copy-start(bf16[3584,64]{0,1:T(8,128)(2,1)} %param.20) | copy-start | bytes 1376260
  14.1 3.8 %copy-start.3 = (bf16[512,1024]{1,0:T(8,128)(2,1)S(1)}, bf16[512,1024]{1,0:T(8,128)(2,1)}, u32[]{:S(2)}) copy-start(bf16[512,1024]{1,0:T(8,128)(2,1)} %param.16) | copy-start | bytes 3145732
  14.1 3.8 %copy-start.6 = (bf16[1024,64]{0,1:T(8,128)(2,1)S(1)}, bf16[1024,64]{0,1:T(8,128)(2,1)}, u32[]{:S(2)}) copy-start(bf16[1024,64]{0,1:T(8,128)(2,1)} %param.21) | copy-start | bytes 393220
  16.0 3.1 %copy-start.7 = (s32[128]{0:T(128)S(1)}, s32[128]{0:T(128)}, u32[]{:S(2)}) copy-start(s32[128]{0:T(128)} %param.11) | copy-start | bytes 1540
  19.0 203.1 %reduce-scatter.2.cloned.1.call-start = ((), (), s32[]{:S(2)}) async-start(), calls=%async_computation.1 | async-start | bytes 405504 | tf_op jit(solution)/shard_map/reduce_scatter | solution.py:62
Sparse Core Ops, SparseCore 0:
  19.1 81.9 all-reduce.2
  109.4 112.6 reduce-scatter.1
where the time goes:
time: 229 us
  waiting for transfers between devices  195 us (85%)
  matrix products  16.8 us (7%)
  between operations  13.5 us (6%)
  other arithmetic  2.35 us (1%)
    reduce_scatter x1, waiting for transfers between devices, body(): lax.psum_scatter(all_three(one_hot, pieces), 'ctx', scatter_dimension=2,...  113 us
    psum x1, waiting for transfers between devices, body(): lax.psum((low_terms[0], low_terms[1], low_terms[2], low_terms[3], low_ter...  81.8 us
    dot_general x5, matrix products, project(): return jnp.dot(data, basis, preferred_element_type=jnp.float32)  11.2 us
    dot_general x3, matrix products, per_group(): jnp.einsum('ta,tb->ab', spread, input_side, precision=lax.Precision.HIGHEST)  5.61 us
  transfers between devices with their start and end apart: 2, of which 2 were waited for; matrix products, arithmetic and copies ran while one was open for 0% of the time, Pallas kernels for 0%

commit v1 on v0

v1 whole, which is shorter than its diff:
```python
import functools

import jax
import jax.numpy as jnp
from jax import lax
from jax.experimental import pallas as pl
from jax.experimental.pallas import tpu as pltpu
from jax.sharding import PartitionSpec as P

K = 64
SAMPLES = 8
BLOCK = 128
LANES = 128
MESH = pl.DeviceIdType.MESH
HIGHEST = lax.Precision.HIGHEST


def project(data_ref, basis_ref):
    return lax.dot_general(
        data_ref[...], basis_ref[...], (((1,), (1,)), ((), ())), preferred_element_type=jnp.float32
    )


def kernel(n_ctx, n_tp, ids, x_in, x_hid, x_gate, x_up, x_out, b_in, b_hid, b_gate, b_up, b_out, result,
           v_in, v_hid, v_gate, v_up, v_out, w_in, w_hid, w_gate, w_up, w_out,
           s_io, s_h, s_gu, r_io, r_h, r_gu, grads, g_send, g_recv, f_recv,
           load_sem, tp_send, tp_recv, ctx_send, ctx_recv, fin_send, fin_recv):
    me_ctx, me_tp = lax.axis_index("ctx"), lax.axis_index("tp")
    own = v_in.shape[0] // n_tp

    loads = []
    pairs = [(x_in, v_in), (b_in, w_in), (x_out, v_out), (b_out, w_out), (x_hid, v_hid), (b_hid, w_hid),
             (x_gate, v_gate), (b_gate, w_gate), (x_up, v_up), (b_up, w_up)]
    for i, (src, dst) in enumerate(pairs):
        load = pltpu.make_async_copy(src, dst, load_sem.at[i])
        load.start()
        loads.append(load)

    barrier = pltpu.get_barrier_semaphore()

    @pl.loop(1, n_tp)
    def _(step):
        pl.semaphore_signal(barrier, inc=1, device_id=(me_ctx, lax.rem(me_tp + step, n_tp)), device_id_type=MESH)

    @pl.loop(1, n_ctx)
    def _(step):
        pl.semaphore_signal(barrier, inc=1, device_id=(lax.rem(me_ctx + step, n_ctx), me_tp), device_id_type=MESH)

    def ready(first):
        loads[first].wait()
        loads[first + 1].wait()

    def exchange(kind, send, recv):
        recv[me_tp] = send[me_tp]

        @pl.loop(1, n_tp)
        def _(step):
            peer = lax.rem(me_tp + step, n_tp)
            pltpu.make_async_remote_copy(
                src_ref=send.at[peer], dst_ref=recv.at[me_tp],
                send_sem=tp_send.at[kind], recv_sem=tp_recv.at[kind],
                device_id=(me_ctx, peer), device_id_type=MESH,
            ).start()

    def finish(kind, send, recv):
        part = recv.at[pl.ds(0, n_tp - 1)]
        pltpu.make_async_copy(part, part, tp_recv.at[kind]).wait()
        part = send.at[pl.ds(0, n_tp - 1)]
        pltpu.make_async_copy(part, part, tp_send.at[kind]).wait()
        total = recv[0]
        for source in range(1, n_tp):
            total = total + recv[source]
        return total

    ready(0)
    low_in = project(v_in, w_in)
    ready(2)
    low_out = project(v_out, w_out)
    s_io[...] = jnp.concatenate([low_in, low_out], axis=1).reshape(s_io.shape)
    pl.semaphore_wait(barrier, n_tp + n_ctx - 2)
    exchange(0, s_io, r_io)

    ready(4)
    low_hid = project(v_hid, w_hid).reshape(n_tp, 2, own // 2, K)
    s_h[...] = jnp.concatenate([low_hid[:, 0], low_hid[:, 1]], axis=2)
    exchange(1, s_h, r_h)

    ready(6)
    low_gate = project(v_gate, w_gate)
    ready(8)
    low_up = project(v_up, w_up)
    s_gu[...] = jnp.concatenate([low_gate, low_up], axis=1).reshape(s_gu.shape)
    exchange(2, s_gu, r_gu)

    in_out = finish(0, s_io, r_io)
    hid_halves = finish(1, s_h, r_h)
    hid = jnp.concatenate([hid_halves[:, :K], hid_halves[:, K:]], axis=0)
    gate_up = finish(2, s_gu, r_gu)

    def outer(output_side, input_side):
        return lax.dot_general(output_side, input_side, (((0,), (0,)), ((), ())), precision=HIGHEST,
                               preferred_element_type=jnp.float32)

    grads[pl.ds(0, 2 * K), :K] = outer(gate_up, in_out[:, :K])
    grads[pl.ds(2 * K, K), :K] = outer(in_out[:, K:], hid)
    even = grads[pl.ds(0, 3 * K // 2, stride=2), :]
    odd = grads[pl.ds(1, 3 * K // 2, stride=2), :]
    both = jnp.concatenate([even[:, :K], odd[:, :K]], axis=1)
    for m in range(3):
        g_send[:, m, :] = both[m * n_ctx:(m + 1) * n_ctx]
    g_recv[me_ctx] = g_send[me_ctx]

    @pl.loop(1, n_ctx)
    def _(step):
        peer = lax.rem(me_ctx + step, n_ctx)
        pltpu.make_async_remote_copy(
            src_ref=g_send.at[peer], dst_ref=g_recv.at[me_ctx],
            send_sem=ctx_send, recv_sem=ctx_recv,
            device_id=(peer, me_tp), device_id_type=MESH,
        ).start()

    part = g_recv.at[pl.ds(0, n_ctx - 1)]
    pltpu.make_async_copy(part, part, ctx_recv).wait()
    part = g_send.at[pl.ds(0, n_ctx - 1)]
    pltpu.make_async_copy(part, part, ctx_send).wait()

    sample = lax.broadcasted_iota(jnp.int32, (SAMPLES, LANES), 0)
    sums = [jnp.zeros((SAMPLES, LANES), jnp.float32) for _ in range(3)]
    blocks = v_in.shape[0] // BLOCK
    mine = me_tp * own // BLOCK
    for source in range(n_ctx):
        chosen = sample == ids[source * blocks + mine]
        for m in range(3):
            row = jnp.broadcast_to(g_recv[source, m:m + 1, :], (SAMPLES, LANES))
            sums[m] = sums[m] + jnp.where(chosen, row, 0.0)
    for m in range(3):
        f_recv[me_tp, m] = sums[m]

    @pl.loop(1, n_tp)
    def _(step):
        peer = lax.rem(me_tp + step, n_tp)
        pltpu.make_async_remote_copy(
            src_ref=f_recv.at[me_tp], dst_ref=f_recv.at[me_tp],
            send_sem=fin_send, recv_sem=fin_recv,
            device_id=(me_ctx, peer), device_id_type=MESH,
        ).start()

    part = f_recv.at[pl.ds(0, n_tp - 1)]
    pltpu.make_async_copy(part, part, fin_recv).wait()
    total = f_recv[0]
    for source in range(1, n_tp):
        total = total + f_recv[source]
    result[...] = total
    pltpu.make_async_copy(part, part, fin_send).wait()


def body(ids, x_in, x_hid, x_gate, x_up, x_out, b_in, b_hid, b_gate, b_up, b_out, *, n_ctx, n_tp):
    tokens, narrow = x_in.shape
    wide = x_hid.shape[1]
    own = tokens // n_tp
    anywhere = pl.BlockSpec(memory_space=pl.ANY)
    f32, bf16 = jnp.float32, jnp.bfloat16
    dma = pltpu.SemaphoreType.DMA
    return pl.pallas_call(
        functools.partial(kernel, n_ctx, n_tp),
        out_shape=jax.ShapeDtypeStruct((3, SAMPLES, LANES), f32),
        in_specs=[pl.BlockSpec(memory_space=pltpu.SMEM)] + [anywhere] * 10,
        out_specs=pl.BlockSpec(memory_space=pltpu.VMEM),
        scratch_shapes=[
            pltpu.VMEM((tokens, narrow), bf16),
            pltpu.VMEM((tokens, wide), bf16),
            pltpu.VMEM((tokens, wide), bf16),
            pltpu.VMEM((tokens, wide), bf16),
            pltpu.VMEM((tokens, narrow), bf16),
            pltpu.VMEM((K, narrow), bf16),
            pltpu.VMEM((K, wide), bf16),
            pltpu.VMEM((K, wide), bf16),
            pltpu.VMEM((K, wide), bf16),
            pltpu.VMEM((K, narrow), bf16),
            pltpu.VMEM((n_tp, own, LANES), f32),
            pltpu.VMEM((n_tp, own // 2, LANES), f32),
            pltpu.VMEM((n_tp, own, LANES), f32),
            pltpu.VMEM((n_tp, own, LANES), f32),
            pltpu.VMEM((n_tp, own // 2, LANES), f32),
            pltpu.VMEM((n_tp, own, LANES), f32),
            pltpu.VMEM((3 * K, LANES), f32),
            pltpu.VMEM((n_ctx, 4, LANES), f32),
            pltpu.VMEM((n_ctx, 4, LANES), f32),
            pltpu.VMEM((n_tp, 3, SAMPLES, LANES), f32),
            dma((10,)), dma((3,)), dma((3,)), dma, dma, dma, dma,
        ],
        compiler_params=pltpu.CompilerParams(
            collective_id=0, has_side_effects=True, vmem_limit_bytes=60 * 1024 * 1024
        ),
    )(ids, x_in, x_hid, x_gate, x_up, x_out, b_in.T, b_hid.T, b_gate.T, b_up.T, b_out.T)


def solution(mesh):
    split, rows = P("ctx", "tp"), P("tp", None)
    return jax.shard_map(
        functools.partial(body, n_ctx=mesh.shape["ctx"], n_tp=mesh.shape["tp"]),
        mesh=mesh,
        in_specs=(P(), split, split, split, split, split, rows, rows, rows, rows, rows),
        out_specs=P(None, None, "ctx"),
        check_vma=False,
    )
```

time: 229 us -> 35.2 us (0.15)
  the two profiles are of different devices: /device:TPU:2 before, /device:TPU:1 now
where the time goes in v1:
time: 35.2 us; the launch traced here: 35 us
  Pallas kernels  33.7 us (96%)
  local copies, waits for them, and re-layouts  1.31 us (4%)
    pallas_call x1, Pallas kernels, body(): pl.pallas_call(functools.partial(kernel, n_ctx, n_tp), out_shape=jax.Shap...  33.7 us
    unnamed x1, local copies, waits for them, and re-layouts  1.31 us

profile of v1, /device:TPU:1, one launch (start us, length us, event | category | flops | bytes accessed | tf_op | source)
XLA Modules:
  0.0 35.0 jit_solution(6237470134172052248)
XLA Ops:
  0.0 33.7 %shard_map.109 = f32[3,8,128]{2,1,0:T(8,128)} custom-call(s32[128]{0:T(128)} %ids.1, bf16[512,1024]{1,0:T(8,128)(2,1)} %x_in.1, bf16[512,3584]{1,0:T(8,128)(2,1)} %x_hid.1, bf16[512,3584]{1,0:T(8,128)(2,1)} %x_gate.1, bf16[512,3584]{1,0:T(8,128)(2,1)} %x_up.1, bf16[512,1024]{1,0:T(8,128)(2,1)} %x_out.1, bf16[64,1024]{1,0:T(8,128)(2,1)} %bitcast.8, ...), custom_call_target="tpu_custom_call" | custom-call | tf_op jit(solution)/shard_map/pallas_call | solution.py:164
  33.7 1.3 %copy.13 = f32[3,8,128]{2,1,0:T(8,128)} copy(f32[3,8,128]{2,1,0:T(8,128)} %shard_map.109) | data formatting | bytes 24576

commit v2 on v1

v2 whole, which is shorter than its diff:
```python
import functools

import jax
import jax.numpy as jnp
from jax import lax
from jax.experimental import pallas as pl
from jax.experimental.pallas import tpu as pltpu
from jax.sharding import PartitionSpec as P

K = 64
SAMPLES = 8
BLOCK = 128
LANES = 128
MESH = pl.DeviceIdType.MESH
HIGHEST = lax.Precision.HIGHEST


def project(data_ref, basis_ref):
    half = data_ref.shape[0] // 2
    basis = basis_ref[...]
    parts = [
        lax.dot_general(
            data_ref[pl.ds(start, half), :], basis, (((1,), (1,)), ((), ())), preferred_element_type=jnp.float32
        )
        for start in (0, half)
    ]
    return jnp.concatenate(parts, axis=0)


def outer(output_side, input_side):
    return lax.dot_general(
        output_side, input_side, (((0,), (0,)), ((), ())), precision=HIGHEST, preferred_element_type=jnp.float32
    )


def wait_bytes(ref, count, sem):
    part = ref.at[pl.ds(0, count)]
    pltpu.make_async_copy(part, part, sem).wait()


def kernel(n_ctx, n_tp, x_ids, x_in, x_hid, x_gate, x_up, x_out, b_in, b_hid, b_gate, b_up, b_out, result,
           ids, v_in, v_hid, v_gate, v_up, v_out, w_in, w_hid, w_gate, w_up, w_out,
           s_io, s_hg, s_u, r_io, r_hg, r_u, grads_go, grads_u, gs_go, gs_u, gr_go, gr_u, f_go, f_u,
           ids_sem, load_sem, tp_send, tp_recv, ctx_send, ctx_recv, fin_send, fin_recv):
    me_ctx, me_tp = lax.axis_index("ctx"), lax.axis_index("tp")
    tokens = v_in.shape[0]
    own = tokens // n_tp

    loads = []

    def load(src, dst):
        copy = pltpu.make_async_copy(src, dst, load_sem.at[len(loads)])
        copy.start()
        loads.append(copy)

    load(x_in, v_in)
    load(b_in, w_in)
    load(x_out, v_out)
    load(b_out, w_out)
    load(x_hid, v_hid)
    load(b_hid, w_hid)

    barrier = pltpu.get_barrier_semaphore()

    @pl.loop(1, n_ctx)
    def _(step):
        pl.semaphore_signal(barrier, inc=1, device_id=(jnp.bitwise_xor(me_ctx, step), me_tp), device_id_type=MESH)

    @pl.loop(1, n_tp)
    def _(step):
        pl.semaphore_signal(barrier, inc=1, device_id=(me_ctx, jnp.bitwise_xor(me_tp, step)), device_id_type=MESH)

    load(x_gate, v_gate)
    load(b_gate, w_gate)
    load(x_up, v_up)
    load(b_up, w_up)
    ids_copy = pltpu.make_async_copy(x_ids, ids, ids_sem)
    ids_copy.start()

    def ready(first):
        loads[first].wait()
        loads[first + 1].wait()

    def tp_exchange(kind, send, recv):
        @pl.loop(1, n_tp)
        def _(step):
            peer = jnp.bitwise_xor(me_tp, step)
            pltpu.make_async_remote_copy(
                src_ref=send.at[peer], dst_ref=recv.at[me_tp],
                send_sem=tp_send.at[kind], recv_sem=tp_recv.at[kind],
                device_id=(me_ctx, peer), device_id_type=MESH,
            ).start()

        recv[me_tp] = send[me_tp]

    def tp_total(kind, recv):
        wait_bytes(recv, n_tp - 1, tp_recv.at[kind])
        total = recv[0]
        for source in range(1, n_tp):
            total = total + recv[source]
        return total

    def ctx_exchange(kind, send, recv):
        @pl.loop(1, n_ctx)
        def _(step):
            peer = jnp.bitwise_xor(me_ctx, step)
            pltpu.make_async_remote_copy(
                src_ref=send.at[peer], dst_ref=recv.at[me_ctx],
                send_sem=ctx_send.at[kind], recv_sem=ctx_recv.at[kind],
                device_id=(peer, me_tp), device_id_type=MESH,
            ).start()

        recv[me_ctx] = send[me_ctx]

    def slices(grads, send, count):
        even = grads[pl.ds(0, count * K // 2, stride=2), :]
        odd = grads[pl.ds(1, count * K // 2, stride=2), :]
        both = jnp.concatenate([even[:, :K], odd[:, :K]], axis=1)
        for m in range(count):
            send[:, m, :] = both[m * n_ctx:(m + 1) * n_ctx]

    def by_sample(kind, recv, out, count):
        wait_bytes(recv, n_ctx - 1, ctx_recv.at[kind])
        sample = lax.broadcasted_iota(jnp.int32, (SAMPLES, LANES), 0)
        sums = [jnp.zeros((SAMPLES, LANES), jnp.float32) for _ in range(count)]
        blocks = tokens // BLOCK
        mine = me_tp * own // BLOCK
        for source in range(n_ctx):
            chosen = sample == ids[source * blocks + mine]
            for m in range(count):
                row = jnp.broadcast_to(recv[source, m:m + 1, :], (SAMPLES, LANES))
                sums[m] = sums[m] + jnp.where(chosen, row, 0.0)
        for m in range(count):
            out[me_tp, m] = sums[m]

        @pl.loop(1, n_tp)
        def _(step):
            peer = jnp.bitwise_xor(me_tp, step)
            pltpu.make_async_remote_copy(
                src_ref=out.at[me_tp], dst_ref=out.at[me_tp],
                send_sem=fin_send.at[kind], recv_sem=fin_recv.at[kind],
                device_id=(me_ctx, peer), device_id_type=MESH,
            ).start()

    def final(kind, out):
        wait_bytes(out, n_tp - 1, fin_recv.at[kind])
        total = out[0]
        for source in range(1, n_tp):
            total = total + out[source]
        return total

    ready(0)
    low_in = project(v_in, w_in)
    ready(2)
    low_out = project(v_out, w_out)
    s_io[...] = jnp.concatenate([low_in, low_out], axis=1).reshape(s_io.shape)
    ready(4)
    low_hid = project(v_hid, w_hid)
    pl.semaphore_wait(barrier, n_tp + n_ctx - 2)
    tp_exchange(0, s_io, r_io)

    ready(6)
    low_gate = project(v_gate, w_gate)
    s_hg[...] = jnp.concatenate([low_hid, low_gate], axis=1).reshape(s_hg.shape)
    tp_exchange(1, s_hg, r_hg)

    ready(8)
    low_up = project(v_up, w_up).reshape(n_tp, 2, own // 2, K)
    s_u[...] = jnp.concatenate([low_up[:, 0], low_up[:, 1]], axis=2)
    tp_exchange(2, s_u, r_u)
    ids_copy.wait()

    in_out = tp_total(0, r_io)
    side_in, side_out = in_out[:, :K], in_out[:, K:]
    hid_gate = tp_total(1, r_hg)
    grads_go[pl.ds(0, K), :K] = outer(hid_gate[:, K:], side_in)
    grads_go[pl.ds(K, K), :K] = outer(side_out, hid_gate[:, :K])
    slices(grads_go, gs_go, 2)
    ctx_exchange(0, gs_go, gr_go)

    up_halves = tp_total(2, r_u)
    grads_u[:, :K] = outer(jnp.concatenate([up_halves[:, :K], up_halves[:, K:]], axis=0), side_in)
    slices(grads_u, gs_u, 1)
    ctx_exchange(1, gs_u, gr_u)

    by_sample(0, gr_go, f_go, 2)
    by_sample(1, gr_u, f_u, 1)
    go = final(0, f_go)
    result[0] = go[0]
    result[2] = go[1]
    result[1] = final(1, f_u)[0]

    for kind, send in enumerate((s_io, s_hg, s_u)):
        wait_bytes(send, n_tp - 1, tp_send.at[kind])
    for kind, send in enumerate((gs_go, gs_u)):
        wait_bytes(send, n_ctx - 1, ctx_send.at[kind])
    for kind, send in enumerate((f_go, f_u)):
        wait_bytes(send, n_tp - 1, fin_send.at[kind])


def body(ids, x_in, x_hid, x_gate, x_up, x_out, b_in, b_hid, b_gate, b_up, b_out, *, n_ctx, n_tp):
    tokens, narrow = x_in.shape
    wide = x_hid.shape[1]
    own = tokens // n_tp
    f32, bf16 = jnp.float32, jnp.bfloat16
    dma = pltpu.SemaphoreType.DMA
    return pl.pallas_call(
        functools.partial(kernel, n_ctx, n_tp),
        out_shape=jax.ShapeDtypeStruct((3, SAMPLES, LANES), f32),
        in_specs=[pl.BlockSpec(memory_space=pl.ANY)] * 11,
        out_specs=pl.BlockSpec(memory_space=pltpu.VMEM),
        scratch_shapes=[
            pltpu.SMEM(ids.shape, jnp.int32),
            pltpu.VMEM((tokens, narrow), bf16),
            pltpu.VMEM((tokens, wide), bf16),
            pltpu.VMEM((tokens, wide), bf16),
            pltpu.VMEM((tokens, wide), bf16),
            pltpu.VMEM((tokens, narrow), bf16),
            pltpu.VMEM((K, narrow), bf16),
            pltpu.VMEM((K, wide), bf16),
            pltpu.VMEM((K, wide), bf16),
            pltpu.VMEM((K, wide), bf16),
            pltpu.VMEM((K, narrow), bf16),
            pltpu.VMEM((n_tp, own, LANES), f32),
            pltpu.VMEM((n_tp, own, LANES), f32),
            pltpu.VMEM((n_tp, own // 2, LANES), f32),
            pltpu.VMEM((n_tp, own, LANES), f32),
            pltpu.VMEM((n_tp, own, LANES), f32),
            pltpu.VMEM((n_tp, own // 2, LANES), f32),
            pltpu.VMEM((2 * K, LANES), f32),
            pltpu.VMEM((K, LANES), f32),
            pltpu.VMEM((n_ctx, 2, LANES), f32),
            pltpu.VMEM((n_ctx, 1, LANES), f32),
            pltpu.VMEM((n_ctx, 2, LANES), f32),
            pltpu.VMEM((n_ctx, 1, LANES), f32),
            pltpu.VMEM((n_tp, 2, SAMPLES, LANES), f32),
            pltpu.VMEM((n_tp, 1, SAMPLES, LANES), f32),
            dma, dma((10,)), dma((3,)), dma((3,)), dma((2,)), dma((2,)), dma((2,)), dma((2,)),
        ],
        compiler_params=pltpu.CompilerParams(
            collective_id=0, has_side_effects=True, vmem_limit_bytes=60 * 1024 * 1024
        ),
    )(ids, x_in, x_hid, x_gate, x_up, x_out, b_in.T, b_hid.T, b_gate.T, b_up.T, b_out.T)


def solution(mesh):
    split, rows = P("ctx", "tp"), P("tp", None)
    return jax.shard_map(
        functools.partial(body, n_ctx=mesh.shape["ctx"], n_tp=mesh.shape["tp"]),
        mesh=mesh,
        in_specs=(P(), split, split, split, split, split, rows, rows, rows, rows, rows),
        out_specs=P(None, None, "ctx"),
        check_vma=False,
    )
```

time: 35.2 us -> 32.9 us (0.935)
  Pallas kernels: 33.7 us -> 31.4 us
    pallas_call x1, Pallas kernels: 33.7 us -> 31.4 us  [body(): pl.pallas_call(functools.partial(kernel, n_ctx, n_tp), out_shape=jax.Shap...]
where the time goes in v2:
time: 32.9 us; the launch traced here: 32.7 us
  Pallas kernels  31.4 us (95%)
  local copies, waits for them, and re-layouts  1.31 us (4%)
    pallas_call x1, Pallas kernels, body(): pl.pallas_call(functools.partial(kernel, n_ctx, n_tp), out_shape=jax.Shap...  31.4 us
    unnamed x1, local copies, waits for them, and re-layouts  1.31 us

profile of v2, /device:TPU:1, one launch (start us, length us, event | category | flops | bytes accessed | tf_op | source)
XLA Modules:
  0.0 32.7 jit_solution(17549668897070762584)
XLA Ops:
  0.0 31.4 %shard_map.109 = f32[3,8,128]{2,1,0:T(8,128)} custom-call(s32[128]{0:T(128)} %x_ids.1, bf16[512,1024]{1,0:T(8,128)(2,1)} %x_in.1, bf16[512,3584]{1,0:T(8,128)(2,1)} %x_hid.1, bf16[512,3584]{1,0:T(8,128)(2,1)} %x_gate.1, bf16[512,3584]{1,0:T(8,128)(2,1)} %x_up.1, bf16[512,1024]{1,0:T(8,128)(2,1)} %x_out.1, bf16[64,1024]{1,0:T(8,128)(2,1)} %bitcast.8, ...), custom_call_target="tpu_custom_call" | custom-call | tf_op jit(solution)/shard_map/pallas_call | solution.py:207
  31.4 1.3 %copy.13 = f32[3,8,128]{2,1,0:T(8,128)} copy(f32[3,8,128]{2,1,0:T(8,128)} %shard_map.109) | data formatting | bytes 24576

commit v3 on v2

--- a/solution.py
+++ b/solution.py
@@ -41,7 +41,7 @@
 def kernel(n_ctx, n_tp, x_ids, x_in, x_hid, x_gate, x_up, x_out, b_in, b_hid, b_gate, b_up, b_out, result,
            ids, v_in, v_hid, v_gate, v_up, v_out, w_in, w_hid, w_gate, w_up, w_out,
            s_io, s_hg, s_u, r_io, r_hg, r_u, grads_go, grads_u, gs_go, gs_u, gr_go, gr_u, f_go, f_u,
-           ids_sem, load_sem, tp_send, tp_recv, ctx_send, ctx_recv, fin_send, fin_recv):
+           ids_sem, load_sem, tp_send, tp_recv, ctx_send, ctx_recv, fin_send, fin_recv, late_sem, all_sem):
     me_ctx, me_tp = lax.axis_index("ctx"), lax.axis_index("tp")
     tokens = v_in.shape[0]
     own = tokens // n_tp
@@ -61,10 +61,21 @@
     load(b_hid, w_hid)
 
     barrier = pltpu.get_barrier_semaphore()
-
-    @pl.loop(1, n_ctx)
-    def _(step):
-        pl.semaphore_signal(barrier, inc=1, device_id=(jnp.bitwise_xor(me_ctx, step), me_tp), device_id_type=MESH)
+    half = n_ctx // 2
+    first_half = me_ctx < half
+
+    def signal_ctx(sem, start):
+        @pl.loop(start, start + half)
+        def _(step):
+            pl.semaphore_signal(sem, inc=1, device_id=(jnp.bitwise_xor(me_ctx, step), me_tp), device_id_type=MESH)
+
+    @pl.when(first_half)
+    def _():
+        signal_ctx(barrier, half)
+
+        @pl.loop(1, half)
+        def _(step):
+            pl.semaphore_signal(barrier, inc=1, device_id=(jnp.bitwise_xor(me_ctx, step), me_tp), device_id_type=MESH)
 
     @pl.loop(1, n_tp)
     def _(step):
@@ -154,10 +165,19 @@
     ready(2)
     low_out = project(v_out, w_out)
     s_io[...] = jnp.concatenate([low_in, low_out], axis=1).reshape(s_io.shape)
+
+    @pl.when(first_half)
+    def _():
+        pl.semaphore_wait(barrier, n_tp - 1 + half - 1)
+
+    @pl.when(jnp.logical_not(first_half))
+    def _():
+        pl.semaphore_wait(barrier, n_tp - 1 + half)
+        signal_ctx(late_sem, half)
+
+    tp_exchange(0, s_io, r_io)
     ready(4)
     low_hid = project(v_hid, w_hid)
-    pl.semaphore_wait(barrier, n_tp + n_ctx - 2)
-    tp_exchange(0, s_io, r_io)
 
     ready(6)
     low_gate = project(v_gate, w_gate)
@@ -169,6 +189,13 @@
     s_u[...] = jnp.concatenate([low_up[:, 0], low_up[:, 1]], axis=2)
     tp_exchange(2, s_u, r_u)
     ids_copy.wait()
+
+    @pl.when(first_half)
+    def _():
+        pl.semaphore_wait(late_sem, half)
+        pl.semaphore_signal(
+            all_sem, inc=1, device_id=(n_ctx - 4 - me_ctx + 2 * lax.rem(me_ctx, 4), me_tp), device_id_type=MESH
+        )
 
     in_out = tp_total(0, r_io)
     side_in, side_out = in_out[:, :K], in_out[:, K:]
@@ -176,6 +203,10 @@
     grads_go[pl.ds(0, K), :K] = outer(hid_gate[:, K:], side_in)
     grads_go[pl.ds(K, K), :K] = outer(side_out, hid_gate[:, :K])
     slices(grads_go, gs_go, 2)
+    @pl.when(jnp.logical_not(first_half))
+    def _():
+        pl.semaphore_wait(all_sem, 1)
+
     ctx_exchange(0, gs_go, gr_go)
 
     up_halves = tp_total(2, r_u)
@@ -203,7 +234,7 @@
     wide = x_hid.shape[1]
     own = tokens // n_tp
     f32, bf16 = jnp.float32, jnp.bfloat16
-    dma = pltpu.SemaphoreType.DMA
+    dma, plain = pltpu.SemaphoreType.DMA, pltpu.SemaphoreType.REGULAR
     return pl.pallas_call(
         functools.partial(kernel, n_ctx, n_tp),
         out_shape=jax.ShapeDtypeStruct((3, SAMPLES, LANES), f32),
@@ -235,7 +266,7 @@
             pltpu.VMEM((n_ctx, 1, LANES), f32),
             pltpu.VMEM((n_tp, 2, SAMPLES, LANES), f32),
             pltpu.VMEM((n_tp, 1, SAMPLES, LANES), f32),
-            dma, dma((10,)), dma((3,)), dma((3,)), dma((2,)), dma((2,)), dma((2,)), dma((2,)),
+            dma, dma((10,)), dma((3,)), dma((3,)), dma((2,)), dma((2,)), dma((2,)), dma((2,)), plain, plain,
         ],
         compiler_params=pltpu.CompilerParams(
             collective_id=0, has_side_effects=True, vmem_limit_bytes=60 * 1024 * 1024

time: 32.9 us -> 31.4 us (0.954)
  Pallas kernels: 31.4 us -> 29.9 us
    pallas_call x1, Pallas kernels: 31.4 us -> 29.9 us  [body(): pl.pallas_call(functools.partial(kernel, n_ctx, n_tp), out_shape=jax.Shap...]
where the time goes in v3:
time: 31.4 us; the launch traced here: 31.2 us
  Pallas kernels  29.9 us (95%)
  local copies, waits for them, and re-layouts  1.31 us (4%)
    pallas_call x1, Pallas kernels, body(): pl.pallas_call(functools.partial(kernel, n_ctx, n_tp), out_shape=jax.Shap...  29.9 us
    unnamed x1, local copies, waits for them, and re-layouts  1.31 us

profile of v3, /device:TPU:1, one launch (start us, length us, event | category | flops | bytes accessed | tf_op | source)
XLA Modules:
  0.0 31.2 jit_solution(15100748586171180436)
XLA Ops:
  0.0 29.9 %shard_map.109 = f32[3,8,128]{2,1,0:T(8,128)} custom-call(s32[128]{0:T(128)} %x_ids.1, bf16[512,1024]{1,0:T(8,128)(2,1)} %x_in.1, bf16[512,3584]{1,0:T(8,128)(2,1)} %x_hid.1, bf16[512,3584]{1,0:T(8,128)(2,1)} %x_gate.1, bf16[512,3584]{1,0:T(8,128)(2,1)} %x_up.1, bf16[512,1024]{1,0:T(8,128)(2,1)} %x_out.1, bf16[64,1024]{1,0:T(8,128)(2,1)} %bitcast.8, ...), custom_call_target="tpu_custom_call" | custom-call | tf_op jit(solution)/shard_map/pallas_call | solution.py:238
  29.9 1.3 %copy.13 = f32[3,8,128]{2,1,0:T(8,128)} copy(f32[3,8,128]{2,1,0:T(8,128)} %shard_map.109) | data formatting | bytes 24576

commit v4 on v3

--- a/solution.py
+++ b/solution.py
@@ -11,8 +11,14 @@
 SAMPLES = 8
 BLOCK = 128
 LANES = 128
+TP_ORDER = (6, 7, 5, 2, 3, 1, 4)
 MESH = pl.DeviceIdType.MESH
 HIGHEST = lax.Precision.HIGHEST
+
+
+def distant(step):
+    z, rest = step // 4, step % 4
+    return (4, 5, 3, 2, 6, 7, 1, 0).index(z), -rest
 
 
 def project(data_ref, basis_ref):
@@ -46,6 +52,12 @@
     tokens = v_in.shape[0]
     own = tokens // n_tp
 
+    barrier = pltpu.get_barrier_semaphore()
+
+    @pl.loop(1, n_tp)
+    def _(step):
+        pl.semaphore_signal(barrier, inc=1, device_id=(me_ctx, jnp.bitwise_xor(me_tp, step)), device_id_type=MESH)
+
     loads = []
 
     def load(src, dst):
@@ -60,7 +72,6 @@
     load(x_hid, v_hid)
     load(b_hid, w_hid)
 
-    barrier = pltpu.get_barrier_semaphore()
     half = n_ctx // 2
     first_half = me_ctx < half
 
@@ -76,10 +87,6 @@
         @pl.loop(1, half)
         def _(step):
             pl.semaphore_signal(barrier, inc=1, device_id=(jnp.bitwise_xor(me_ctx, step), me_tp), device_id_type=MESH)
-
-    @pl.loop(1, n_tp)
-    def _(step):
-        pl.semaphore_signal(barrier, inc=1, device_id=(me_ctx, jnp.bitwise_xor(me_tp, step)), device_id_type=MESH)
 
     load(x_gate, v_gate)
     load(b_gate, w_gate)
@@ -93,8 +100,7 @@
         loads[first + 1].wait()
 
     def tp_exchange(kind, send, recv):
-        @pl.loop(1, n_tp)
-        def _(step):
+        for step in TP_ORDER:
             peer = jnp.bitwise_xor(me_tp, step)
             pltpu.make_async_remote_copy(
                 src_ref=send.at[peer], dst_ref=recv.at[me_tp],
@@ -112,8 +118,7 @@
         return total
 
     def ctx_exchange(kind, send, recv):
-        @pl.loop(1, n_ctx)
-        def _(step):
+        for step in sorted(range(1, n_ctx), key=distant):
             peer = jnp.bitwise_xor(me_ctx, step)
             pltpu.make_async_remote_copy(
                 src_ref=send.at[peer], dst_ref=recv.at[me_ctx],
@@ -144,8 +149,7 @@
         for m in range(count):
             out[me_tp, m] = sums[m]
 
-        @pl.loop(1, n_tp)
-        def _(step):
+        for step in TP_ORDER:
             peer = jnp.bitwise_xor(me_tp, step)
             pltpu.make_async_remote_copy(
                 src_ref=out.at[me_tp], dst_ref=out.at[me_tp],

time: 31.4 us -> 30.6 us (0.975)
  Pallas kernels: 29.9 us -> 29.2 us
    pallas_call x1, Pallas kernels: 29.9 us -> 29.2 us  [body(): pl.pallas_call(functools.partial(kernel, n_ctx, n_tp), out_shape=jax.Shap...]
where the time goes in v4:
time: 30.6 us; the launch traced here: 30.5 us
  Pallas kernels  29.2 us (95%)
  local copies, waits for them, and re-layouts  1.31 us (4%)
    pallas_call x1, Pallas kernels, body(): pl.pallas_call(functools.partial(kernel, n_ctx, n_tp), out_shape=jax.Shap...  29.2 us
    unnamed x1, local copies, waits for them, and re-layouts  1.31 us

profile of v4, /device:TPU:1, one launch (start us, length us, event | category | flops | bytes accessed | tf_op | source)
XLA Modules:
  0.0 30.5 jit_solution(14374651628250426854)
XLA Ops:
  0.0 29.2 %shard_map.109 = f32[3,8,128]{2,1,0:T(8,128)} custom-call(s32[128]{0:T(128)} %x_ids.1, bf16[512,1024]{1,0:T(8,128)(2,1)} %x_in.1, bf16[512,3584]{1,0:T(8,128)(2,1)} %x_hid.1, bf16[512,3584]{1,0:T(8,128)(2,1)} %x_gate.1, bf16[512,3584]{1,0:T(8,128)(2,1)} %x_up.1, bf16[512,1024]{1,0:T(8,128)(2,1)} %x_out.1, bf16[64,1024]{1,0:T(8,128)(2,1)} %bitcast.8, ...), custom_call_target="tpu_custom_call" | custom-call | tf_op jit(solution)/shard_map/pallas_call | solution.py:242
  29.2 1.3 %copy.13 = f32[3,8,128]{2,1,0:T(8,128)} copy(f32[3,8,128]{2,1,0:T(8,128)} %shard_map.109) | data formatting | bytes 24576

commit v5 on v4

--- a/solution.py
+++ b/solution.py
@@ -34,8 +34,15 @@
 
 
 def outer(output_side, input_side):
+    wide, narrow = zip(*[
+        (side.astype(jnp.bfloat16), (side - side.astype(jnp.bfloat16).astype(jnp.float32)).astype(jnp.bfloat16))
+        for side in (output_side, input_side)
+    ])
     return lax.dot_general(
-        output_side, input_side, (((0,), (0,)), ((), ())), precision=HIGHEST, preferred_element_type=jnp.float32
+        jnp.concatenate([wide[0], wide[0], narrow[0]], axis=0),
+        jnp.concatenate([wide[1], narrow[1], wide[1]], axis=0),
+        (((0,), (0,)), ((), ())),
+        preferred_element_type=jnp.float32,
     )
 
 
@@ -54,8 +61,7 @@
 
     barrier = pltpu.get_barrier_semaphore()
 
-    @pl.loop(1, n_tp)
-    def _(step):
+    for step in TP_ORDER:
         pl.semaphore_signal(barrier, inc=1, device_id=(me_ctx, jnp.bitwise_xor(me_tp, step)), device_id_type=MESH)
 
     loads = []
@@ -76,8 +82,7 @@
     first_half = me_ctx < half
 
     def signal_ctx(sem, start):
-        @pl.loop(start, start + half)
-        def _(step):
+        for step in sorted(range(start, start + half), key=distant):
             pl.semaphore_signal(sem, inc=1, device_id=(jnp.bitwise_xor(me_ctx, step), me_tp), device_id_type=MESH)
 
     @pl.when(first_half)

time: 30.6 us -> 30.6 us (level)
  no operation moved by 1% of the time
where the time goes in v5:
time: 30.6 us; the launch traced here: 30.4 us
  Pallas kernels  29.1 us (95%)
  local copies, waits for them, and re-layouts  1.31 us (4%)
    pallas_call x1, Pallas kernels, body(): pl.pallas_call(functools.partial(kernel, n_ctx, n_tp), out_shape=jax.Shap...  29.1 us
    unnamed x1, local copies, waits for them, and re-layouts  1.31 us

profile of v5, /device:TPU:1, one launch (start us, length us, event | category | flops | bytes accessed | tf_op | source)
XLA Modules:
  0.0 30.4 jit_solution(13987351691132009552)
XLA Ops:
  0.0 29.1 %shard_map.109 = f32[3,8,128]{2,1,0:T(8,128)} custom-call(s32[128]{0:T(128)} %x_ids.1, bf16[512,1024]{1,0:T(8,128)(2,1)} %x_in.1, bf16[512,3584]{1,0:T(8,128)(2,1)} %x_hid.1, bf16[512,3584]{1,0:T(8,128)(2,1)} %x_gate.1, bf16[512,3584]{1,0:T(8,128)(2,1)} %x_up.1, bf16[512,1024]{1,0:T(8,128)(2,1)} %x_out.1, bf16[64,1024]{1,0:T(8,128)(2,1)} %bitcast.8, ...), custom_call_target="tpu_custom_call" | custom-call | tf_op jit(solution)/shard_map/pallas_call | solution.py:247
  29.1 1.3 %copy.13 = f32[3,8,128]{2,1,0:T(8,128)} copy(f32[3,8,128]{2,1,0:T(8,128)} %shard_map.109) | data formatting | bytes 24576
